TPU v7x, 32 devices: a whole 2x2x4 slice. The times are simulated.
32 devices in a mesh: seq: 8 (over z, y), head: 4 (over x, core).
Axes of the slice: x: 2, y: 2, z: 4, core: 2. Of those that a mesh axis runs over, the one named last changes fastest.
Arguments:
- mamba_inner: bfloat16 [1024, 3072], P('seq', 'head'), may hold values from -6 to 6
- mamba_groups: bfloat16 [1024, 512], P('seq'), may hold values from -6 to 6
- selective_gate: bfloat16 [1024, 3072], P('seq', 'head'), may hold values from -6 to 6
- step_raw: float32 [48, 1024], P('head', 'seq'), may hold values from -3 to 3
- step_bias: float32 [48], P('head'), may hold values from -0.5 to 0.5
- decay_log: float32 [48], P('head'), may hold values from -12 to -2
- conv_inner: float32 [4, 3072], P(None, 'head'), may hold values from -3 to 3
- conv_groups: float32 [4, 512], replicated, may hold values from -3 to 3
- gated_norm_gain: float32 [3072], P('head'), may hold values from 0.1 to 1.9
- query_rows: bfloat16 [1024, 1024], P('seq', 'head'), may hold values from -8 to 8
- key_rows: bfloat16 [1024, 256], P('seq'), may hold values from -8 to 8
- value_rows: bfloat16 [1024, 256], P('seq'), may hold values from -6 to 6
- segment_ids: int32 [1024], P('seq'), may hold values from 0 to 15, never falling along the last dimension, each value on 1 to 682 neighbouring positions
- mamba_proj: bfloat16 [3072, 2048], P('head'), may hold values from -0.109375 to 0.109375
- attn_proj: bfloat16 [1024, 2048], P('head'), may hold values from -0.1875 to 0.1875
Outputs:
- mixed: bfloat16 [1024, 2048], P('seq', 'head')
Inputs may be any that keep to these rules, and one draw needn't show every extreme that they name: `segment_ids`: prompt numbers never fall along the tokens; each prompt holds 1 to 682 tokens and one holds exactly 682.
All inputs are finite; a program needn't handle non-finite values.
Results may differ from a plain program's by a relative error of at most 0.015.
Values may be sent and summed in bfloat16 or wider, within the bound.
A program may use at most 128 MiB of HBM per device.

v0:
```python
import math
import jax
import jax.numpy as jnp
from jax import lax
from jax.sharding import PartitionSpec as P

HEAD_CHANNELS = 64
STATE_SIZE = 256
QH = 8
KVH = 2
HD = 128


def shifted(value, axis, steps):
    count = lax.axis_size(axis)
    first, last = (max(0, -steps), min(count, count - steps))
    return lax.ppermute(value, axis, [(source, source + steps) for source in range(first, last)])


def entering(array, axis, combine, identity):
    length, position = (lax.axis_size(axis), lax.axis_index(axis))
    everything = jax.tree.map(
        lambda part, kind: lax.all_gather(part.astype(kind), axis),
        array,
        (jnp.bfloat16, jnp.bfloat16),
    )
    start = jax.tree.map(
        lambda part, zero: jnp.broadcast_to(jnp.asarray(zero, part.dtype), part.shape),
        array,
        identity,
    )

    def turn(k, before):
        reached = k < position
        new = combine(
            before, jax.tree.map(lambda part, own: part[k].astype(own.dtype), everything, array)
        )
        return jax.tree.map(lambda a, b: jnp.where(reached, a, b), new, before)

    return lax.fori_loop(0, length, turn, start)


def conv_silu(rows, weight, segs, rim_rows, rim_segs):
    item_count = rows.shape[0]
    padded = jnp.concatenate([rim_rows.astype(jnp.float32), rows.astype(jnp.float32)], 0)
    seg_pad = jnp.concatenate([rim_segs, segs], 0)
    total = jnp.zeros(rows.shape, jnp.float32)
    for offset in range(weight.shape[0]):
        window = padded[offset : offset + item_count]
        keep = (seg_pad[offset : offset + item_count] == segs).astype(jnp.float32)
        total = total + weight[offset][None, :] * window * keep[:, None]
    return jax.nn.silu(total).astype(jnp.bfloat16)


def mamba_local(inner, groups, segs, steps, rates, prev_last):
    highest = lax.Precision.HIGHEST
    cumul = jnp.cumsum(-steps * rates[:, None], axis=1)
    read_b = groups[:, :STATE_SIZE]
    read_c = groups[:, STATE_SIZE:]
    intersection = jnp.dot(read_c, read_b.T, preferred_element_type=jnp.float32)
    order = jnp.arange(segs.shape[0], dtype=jnp.int32)
    live = (segs[:, None] == segs[None, :]) & (order[:, None] >= order[None, :])
    decays = jnp.exp(jnp.where(live[None], cumul[:, :, None] - cumul[:, None, :], -jnp.inf))
    mixing = intersection[None] * decays
    scaled = inner.astype(jnp.float32) * steps.T[:, :, None]
    output = jnp.einsum("htj,jhd->thd", mixing, scaled, precision=highest)
    tail = jnp.exp(cumul[:, -1:] - cumul) * (segs == segs[-1]).astype(jnp.float32)[None, :]
    local_state = jnp.einsum(
        "ht,thd,tn->hdn", tail, scaled, read_b.astype(jnp.float32), precision=highest
    )
    through = jnp.exp(cumul[:, -1]) * (segs[-1] == prev_last).astype(jnp.float32)
    return (output, through, local_state, cumul)


def mamba_incoming(output, incoming, groups, segs, cumul, prev_last):
    read_c = groups[:, STATE_SIZE:].astype(jnp.float32)
    joined = (segs == prev_last).astype(jnp.float32)
    from_carry = jnp.einsum("hdn,tn->thd", incoming, read_c, precision=lax.Precision.HIGHEST)
    return output + jnp.exp(cumul).T[:, :, None] * joined[:, None, None] * from_carry


def combine_states(earlier, later):
    return (earlier[0] * later[0], later[0][:, None, None] * earlier[1] + later[1])


def shards(
    mamba_inner,
    mamba_groups,
    selective_gate,
    step_raw,
    step_bias,
    decay_log,
    conv_inner,
    conv_groups,
    gated_norm_gain,
    query_rows,
    key_rows,
    value_rows,
    segment_ids,
    mamba_proj,
    attn_proj,
):
    item_count = segment_ids.shape[0]
    taps = conv_inner.shape[0]
    resident_heads = step_raw.shape[0]
    rim_inner, rim_groups, rim_marks = shifted(
        (
            mamba_inner[item_count - taps + 1 :],
            mamba_groups[item_count - taps + 1 :],
            segment_ids[item_count - taps + 1 :].astype(jnp.bfloat16),
        ),
        "seq",
        1,
    )
    rim_segs = rim_marks.astype(jnp.float32).astype(jnp.int32)
    prev_last = rim_segs[-1]
    inner_filtered = conv_silu(mamba_inner, conv_inner, segment_ids, rim_inner, rim_segs).reshape(
        item_count, resident_heads, HEAD_CHANNELS
    )
    groups_conv = conv_silu(mamba_groups, conv_groups, segment_ids, rim_groups, rim_segs)
    steps = jax.nn.softplus(step_raw + step_bias[:, None])
    rates = jnp.exp(decay_log)
    output, through, local_state, cumul = mamba_local(
        inner_filtered, groups_conv, segment_ids, steps, rates, prev_last
    )
    identity = (jnp.ones_like(through), jnp.zeros_like(local_state))
    carry_decay, carry_state = entering((through, local_state), "seq", combine_states, identity)
    selective_output = mamba_incoming(
        output, carry_state, groups_conv, segment_ids, cumul, prev_last
    )
    gated_values = selective_output * jax.nn.silu(selective_gate.astype(jnp.float32)).reshape(
        item_count, resident_heads, HEAD_CHANNELS
    )
    mean_square = jnp.mean(gated_values * gated_values, axis=-1, keepdims=True)
    normalized_rows = (
        (
            gated_values
            * lax.rsqrt(mean_square + 1e-05)
            * gated_norm_gain.reshape(resident_heads, HEAD_CHANNELS)
        )
        .astype(jnp.bfloat16)
        .reshape(item_count, resident_heads * HEAD_CHANNELS)
    )
    heads_here = query_rows.shape[1] // HD
    group_size = QH // KVH
    kv_index = lax.axis_index("head") * heads_here // group_size
    my_keys = lax.dynamic_slice_in_dim(key_rows, kv_index * HD, HD, 1)
    my_values = lax.dynamic_slice_in_dim(value_rows, kv_index * HD, HD, 1)
    marks = segment_ids.astype(jnp.bfloat16)
    block_start = lax.axis_index("seq") * item_count
    query_pos = block_start + jnp.arange(item_count, dtype=jnp.int32)
    queries = query_rows.reshape(item_count, heads_here, HD).transpose(1, 0, 2)
    scale = 1.0 / math.sqrt(HD)
    start_state = (
        jnp.full((heads_here, item_count), -1e30, jnp.float32),
        jnp.zeros((heads_here, item_count), jnp.float32),
        jnp.zeros((heads_here, item_count, HD), jnp.float32),
    )
    piece_keys = lax.all_gather(my_keys, "seq", axis=0, tiled=True)
    piece_values = lax.all_gather(my_values, "seq", axis=0, tiled=True)
    piece_marks = lax.all_gather(marks, "seq", axis=0, tiled=True)
    rows = piece_keys.shape[0]
    width = math.gcd(rows, item_count)
    blocks = rows // width

    def one_block(state, item):
        top, total, summed = state
        block_keys, block_values, block_marks, offset = item
        key_pos = offset * width + jnp.arange(width, dtype=jnp.int32)
        key_seg = block_marks.astype(jnp.float32).astype(jnp.int32)
        allowed = (
            (key_seg[None, :] == segment_ids[:, None])
            & (key_pos[None, :] <= query_pos[:, None])
            & (key_pos[None, :] >= 0)
        )
        scores = (
            jnp.einsum("hqd,kd->hqk", queries, block_keys, preferred_element_type=jnp.float32)
            * scale
        )
        scores = jnp.where(allowed[None], scores, -jnp.inf)
        new_top = jnp.maximum(top, jnp.max(scores, axis=-1))
        rescale = jnp.exp(top - new_top)
        weights = jnp.exp(scores - new_top[..., None])
        total = total * rescale + jnp.sum(weights, axis=-1)
        summed = summed * rescale[..., None] + jnp.einsum(
            "hqk,kd->hqd",
            weights.astype(jnp.bfloat16),
            block_values,
            preferred_element_type=jnp.float32,
        )
        return ((new_top, total, summed), None)

    items = (
        piece_keys.reshape(blocks, width, HD),
        piece_values.reshape(blocks, width, HD),
        piece_marks.reshape(blocks, width),
        jnp.arange(blocks, dtype=jnp.int32),
    )
    result, unused = lax.scan(one_block, start_state, items)
    top_final, total_final, summed_final = result
    attended = (
        (summed_final / total_final[..., None])
        .astype(jnp.bfloat16)
        .transpose(1, 0, 2)
        .reshape(item_count, heads_here * HD)
    )
    terms = jnp.dot(normalized_rows, mamba_proj, preferred_element_type=jnp.float32) + jnp.dot(
        attended, attn_proj, preferred_element_type=jnp.float32
    )
    return lax.psum_scatter(terms.astype(jnp.bfloat16), "head", scatter_dimension=1, tiled=True)


def solution(mesh):
    placed = (
        P("seq", "head"),
        P("seq", None),
        P("seq", "head"),
        P("head", "seq"),
        P("head"),
        P("head"),
        P(None, "head"),
        P(),
        P("head"),
        P("seq", "head"),
        P("seq", None),
        P("seq", None),
        P("seq"),
        P("head", None),
        P("head", None),
    )
    return jax.shard_map(
        shards, mesh=mesh, in_specs=placed, out_specs=P("seq", "head"), check_vma=False
    )
```

profile of v0, /device:TPU:0, one launch (start us, length us, event | category | flops | bytes accessed | tf_op | source)
XLA Modules:
  0.0 241.9 jit_solution(1705443980735956197)
XLA Ops:
  6.5 0.8 fusion.75
  7.9 5.4 %collective-permute-start.1 = (bf16[3]{0:T(256)(128)(2,1)}, bf16[3]{0:T(256)(128)(2,1)}, u32[]{:S(2)}, u32[]{:S(2)}) collective-permute-start(bf16[3]{0:T(256)(128)(2,1)} %slice.85), channel_id=1, source_target_pairs={{0,4},{4,8},{8,12},{12,16},{16,20},{20,24},{24,28},{1,5},{5,9},{9,... | collective-permute-start | bytes 26 | tf_op jit(solution)/shard_map/ppermute | solution.py:17
  13.3 0.7 slice.95
  14.0 3.5 %collective-permute-start.2 = (bf16[3,512]{1,0:T(4,128)(2,1)S(1)}, bf16[3,512]{1,0:T(4,128)(2,1)}, u32[]{:S(2)}, u32[]{:S(2)}) collective-permute-start(bf16[3,512]{1,0:T(4,128)(2,1)S(1)} %slice.95), channel_id=1, source_target_pairs={{0,4},{4,8},{8,12},{12,16},{16,20},{20,24},{24,28},{1,5},{5,9},{9,... | collective-permute-start | bytes 9224 | tf_op jit(solution)/shard_map/ppermute | solution.py:17
  17.5 0.7 slice.83
  18.2 0.8 copy.27
  19.1 3.5 %collective-permute-start = (bf16[3,768]{0,1:T(8,128)(2,1)}, bf16[3,768]{0,1:T(8,128)(2,1)}, u32[]{:S(2)}, u32[]{:S(2)}) collective-permute-start(bf16[3,768]{0,1:T(8,128)(2,1)} %copy.27), channel_id=1, source_target_pairs={{0,4},{4,8},{8,12},{12,16},{16,20},{20,24},{24,28},{1,5},{5,9},{9,... | collective-permute-start | bytes 13832 | tf_op jit(solution)/shard_map/ppermute | solution.py:17
  22.6 1.2 slice.106
  23.8 1.6 convert_element_type.131
  25.5 1.1 copy.28
  26.6 0.9 fusion.74
  27.5 0.9 slice_reduce_fusion.4
  28.4 0.8 convert_element_type.121
  29.8 0.8 fusion.71
  31.1 0.8 constant_dynamic-slice_fusion.2
  31.8 32.9 %all_gather.23 = bf16[1024,128]{1,0:T(8,128)(2,1)} all-gather(bf16[128,128]{1,0:T(8,128)(2,1)S(1)} %constant_dynamic-slice_fusion.2), channel_id=1, replica_groups=mesh['seq'=8,'head'=4] {'seq'}, dimensions={0}, use_global_device_ids=true | all-gather | bytes 294912 | tf_op jit(solution)/shard_map/all_gather | solution.py:159
  64.8 0.8 constant_dynamic-slice_fusion.1
  65.5 32.9 %all_gather.24 = bf16[1024,128]{1,0:T(8,128)(2,1)} all-gather(bf16[128,128]{1,0:T(8,128)(2,1)S(1)} %constant_dynamic-slice_fusion.1), channel_id=1, replica_groups=mesh['seq'=8,'head'=4] {'seq'}, dimensions={0}, use_global_device_ids=true | all-gather | bytes 294912 | tf_op jit(solution)/shard_map/all_gather | solution.py:160
  98.4 16.8 %all-gather.2 = bf16[8,1,128]{2,1,0:T(2,128)(2,1)S(1)} all-gather(bf16[1,1,128]{2,1,0:T(2,128)(2,1)S(1)} %get-tuple-element.295), channel_id=1, replica_groups=mesh['seq'=8,'head'=4] {'seq'}, dimensions={0}, use_global_device_ids=true | all-gather | bytes 2304 | tf_op jit(solution)/shard_map/all_gather | solution.py:161
  115.8 0.9 copy.30
  118.1 0.7 pad_add_fusion
  118.8 2.0 compare_convert_fusion.4
  122.1 1.6 multiply_convert_fusion.2
  123.7 1.0 convert_element_type.120
  124.7 2.5 %multiply_convert_fusion.1 = bf16[128,768]{0,1:T(8,128)(2,1)S(1)} fusion(f32[128,768]{0,1:T(8,128)} %convert_element_type.121, f32[3,768]{0,1:T(8,128)S(1)} %convert_element_type.120, f32[768]{0:T(1024)S(1)} %get-tuple-element.241, f32[128]{0:T(128)S(1)} %get-tuple-element.290, f32[768]{0:T(1024)S(1)} %get-tuple-element.242, f32[128]{0:T(128)S(1)} %get-tuple-element.291, ...), kind=kLoop, calls=%fused_computation.74 | loop fusion | flops 1769472 | bytes 612864 | tf_op jit(solution)/shard_map/convert_element_type | solution.py:52
  127.9 1.2 convolution_convert_fusion
  129.2 32.5 %while.30 = (s32[]{:T(128)}, f32[2,128]{1,0:T(2,128)S(1)}, f32[2,128]{1,0:T(2,128)S(1)}, f32[2,128,128]{2,1,0:T(8,128)S(1)}, bf16[8,128]{1,0:T(8,128)(2,1)}, /*i...) while((s32[]{:T(128)}, f32[2,128]{1,0:T(2,128)S(1)}, ...), condition=%wide.region_7.8_spmd.clone, body=%wide.region_4.7_spmd.clone.sunk | while | flops 17172484 | bytes 840889 | solution.py:199
  130.4 0.7 fusion.96
  131.2 0.9 fusion.97
  132.2 1.0 convolution_add_fusion.3
  134.5 0.7 fusion.96
  135.3 0.9 fusion.97
  136.3 1.0 convolution_add_fusion.3
  139.3 0.9 fusion.97
  140.4 1.0 convolution_add_fusion.3
  143.4 0.9 fusion.97
  144.4 1.0 convolution_add_fusion.3
  146.6 0.7 fusion.96
  147.4 0.9 fusion.97
  148.5 1.0 convolution_add_fusion.3
  151.5 0.9 fusion.97
  152.5 1.0 convolution_add_fusion.3
  155.6 0.9 fusion.97
  156.6 1.0 convolution_add_fusion.3
  159.6 1.0 fusion.97
  160.7 1.0 convolution_add_fusion.3
  161.7 1.8 copy.29
  164.3 1.3 dynamic-slice
  166.4 1.8 convert_multiply_fusion
  168.2 2.6 %fusion.76 = f32[128,2048]{1,0:T(8,128)} fusion(bf16[128,256]{0,1:T(8,128)(2,1)S(1)} %bitcast.93, bf16[256,2048]{1,0:T(8,128)(2,1)} %param.33), kind=kOutput, calls=%fused_computation.132 | convolution fusion | flops 134217728 | bytes 2162688 | tf_op jit(solution)/shard_map/dot_general | solution.py:207
  172.5 18.7 %all-reduce = bf16[96]{0:T(256)(128)(2,1)S(1)} all-reduce(bf16[96]{0:T(256)(128)(2,1)S(1)} %dynamic-update-slice), channel_id=2, replica_groups=mesh['seq'=8,'head'=4] {'seq'}, use_global_device_ids=true, to_apply=%add | all-reduce | flops 96 | bytes 384
  191.4 18.2 %while.29 = (s32[]{:T(128)}, f32[12,64,256]{2,1,0:T(8,128)}, s32[]{:T(128)}, bf16[8,12]{1,0:T(8,128)(2,1)S(1)}, bf16[8,12,64,256]{3,2,1,0:T(8,128)(2,1)}, /*index=5*/s32[]{:T(128)}, s32[]{:T(128)}) while((s32[]{:T(128)}, f32[12,64,256]{2,1,0:T(8,128)}, s32[]{:T(128)}, bf16[8,12]{1,0:T(8,128)(2,1)S(1)}, ...), condition=%wide.region_2.3_spmd.clone, body=%wide.region_1.2_spmd.clone.sunk | while | flops 983056 | bytes 1966305 | solution.py:40
  191.5 2.1 fusion.92
  193.5 2.3 fusion.92
  195.8 2.3 fusion.92
  198.1 2.3 fusion.92
  200.4 2.3 fusion.92
  202.7 2.3 fusion.92
  205.0 2.3 fusion.92
  207.3 2.3 fusion.92
  209.6 1.7 convolution_multiply_fusion.1
  211.3 2.8 %multiply_reduce_fusion = (f32[128,12]{0,1:T(8,128)S(1)}, f32[128,12,64]{0,2,1:T(8,128)S(1)}) fusion(f32[128,12,64]{0,2,1:T(8,128)} %bitcast.92, f32[128,12,64]{0,2,1:T(8,128)S(1)} %convolution_multiply_fusion.1, f32[12,128]{1,0:T(8,128)S(1)} %reduce_window_sum.11, f32[128,128]{1,0:T(8,128)S(1)} %fusion.66, pred[128,128]{1,0:T(8,128)(4,1)S(1)} %fusion.64, ...), kind=kOutput, calls=%fused_computation.69 | convolution fusion | flops 152173056 | bytes 1476608 | tf_op jit(solution)/shard_map/htj,jhd->thd/dot_general | solution.py:66
  214.4 1.4 fusion.20
  215.8 19.3 %reduce-scatter.2.cloned.1.call-done = bf16[128,512]{1,0:T(8,128)(2,1)} async-done(((bf16[128,2048]{1,0:T(8,128)(2,1)}), bf16[128,512]{1,0:T(8,128)(2,1)}) %reduce-scatter.2.cloned.1.call-update) | async-done | bytes 131088 | tf_op jit(solution)/shard_map/reduce_scatter | solution.py:210
  (133 shorter events, 17.3 us)
Async XLA Ops:
  6.5 207.8 %copy-start = (bf16[768,2048]{1,0:T(8,128)(2,1)S(1)}, bf16[768,2048]{1,0:T(8,128)(2,1)}, u32[]{:S(2)}) copy-start(bf16[768,2048]{1,0:T(8,128)(2,1)} %param.32) | copy-start | bytes 9437188
  6.5 122.6 %copy-start.5 = (s32[128]{0:T(128)S(1)}, s32[128]{0:T(128)}, u32[]{:S(2)}) copy-start(s32[128]{0:T(128)} %param.31) | copy-start | bytes 1540
  6.5 184.9 %all-gather.5.cloned.1.call-start = ((), (), s32[]{:S(2)}) async-start(), calls=%async_computation.2 | async-start | bytes 3538944 | tf_op jit(solution)/shard_map/all_gather | solution.py:23
  7.9 108.9 %collective-permute-start.1 = (bf16[3]{0:T(256)(128)(2,1)}, bf16[3]{0:T(256)(128)(2,1)}, u32[]{:S(2)}, u32[]{:S(2)}) collective-permute-start(bf16[3]{0:T(256)(128)(2,1)} %slice.85), channel_id=1, source_target_pairs={{0,4},{4,8},{8,12},{12,16},{16,20},{20,24},{24,28},{1,5},{5,9},{9,... | collective-permute-start | bytes 26 | tf_op jit(solution)/shard_map/ppermute | solution.py:17
  14.0 107.4 %collective-permute-start.2 = (bf16[3,512]{1,0:T(4,128)(2,1)S(1)}, bf16[3,512]{1,0:T(4,128)(2,1)}, u32[]{:S(2)}, u32[]{:S(2)}) collective-permute-start(bf16[3,512]{1,0:T(4,128)(2,1)S(1)} %slice.95), channel_id=1, source_target_pairs={{0,4},{4,8},{8,12},{12,16},{16,20},{20,24},{24,28},{1,5},{5,9},{9,... | collective-permute-start | bytes 9224 | tf_op jit(solution)/shard_map/ppermute | solution.py:17
  19.1 104.6 %collective-permute-start = (bf16[3,768]{0,1:T(8,128)(2,1)}, bf16[3,768]{0,1:T(8,128)(2,1)}, u32[]{:S(2)}, u32[]{:S(2)}) collective-permute-start(bf16[3,768]{0,1:T(8,128)(2,1)} %copy.27), channel_id=1, source_target_pairs={{0,4},{4,8},{8,12},{12,16},{16,20},{20,24},{24,28},{1,5},{5,9},{9,... | collective-permute-start | bytes 13832 | tf_op jit(solution)/shard_map/ppermute | solution.py:17
  30.6 98.6 %copy-start.6 = (f32[128,12]{0,1:T(8,128)}, f32[128,12]{0,1:T(8,128)S(1)}, u32[]{:S(2)}) copy-start(f32[128,12]{0,1:T(8,128)S(1)} %get-tuple-element.281) | copy-start | bytes 18436
  123.7 3.5 %copy-start.2 = (bf16[128,512]{1,0:T(8,128)(2,1)}, bf16[128,512]{1,0:T(8,128)(2,1)S(1)}, u32[]{:S(2)}) copy-start(bf16[128,512]{1,0:T(8,128)(2,1)S(1)} %multiply_convert_fusion.2) | copy-start | bytes 393220
  127.2 0.7 copy-start.4
  127.2 36.3 %copy-start.10 = (f32[768]{0:T(1024)S(1)}, f32[768]{0:T(1024)}, u32[]{:S(2)}) copy-start(f32[768]{0:T(1024)} %param.27) | copy-start | bytes 9220
  129.1 106.0 %reduce-scatter.2.cloned.1.call-start = ((), (), s32[]{:S(2)}) async-start(), calls=%async_computation.1 | async-start | bytes 655360 | tf_op jit(solution)/shard_map/reduce_scatter | solution.py:210
  161.7 29.6 %copy-start.3 = (bf16[128,512]{1,0:T(8,128)(2,1)S(1)}, bf16[128,512]{1,0:T(8,128)(2,1)}, u32[]{:S(2)}) copy-start(bf16[128,512]{1,0:T(8,128)(2,1)} %copy-done.2) | copy-start | bytes 393220
  191.4 18.2 %copy-start.8 = (f32[128,12]{0,1:T(8,128)S(1)}, f32[128,12]{0,1:T(8,128)}, u32[]{:S(2)}) copy-start(f32[128,12]{0,1:T(8,128)} %get-tuple-element.283) | copy-start | bytes 18436
  191.4 19.9 %copy-start.7 = (f32[128,12]{0,1:T(8,128)S(1)}, f32[128,12]{0,1:T(8,128)}, u32[]{:S(2)}) copy-start(f32[128,12]{0,1:T(8,128)} %copy-done.6) | copy-start | bytes 18436
  191.4 22.7 %copy-start.9 = (f32[12,64]{1,0:T(8,128)S(1)}, f32[12,64]{1,0:T(8,128)}, u32[]{:S(2)}) copy-start(f32[12,64]{1,0:T(8,128)} %mul.345) | copy-start | bytes 9220
  209.6 4.7 %copy-start.1 = (f32[128,2048]{1,0:T(8,128)S(1)}, f32[128,2048]{1,0:T(8,128)}, u32[]{:S(2)}) copy-start(f32[128,2048]{1,0:T(8,128)} %fusion.76) | copy-start | bytes 3145732
Sparse Core Ops, SparseCore 0:
  129.2 58.6 all-gather.4
  215.9 19.1 reduce-scatter.1
where the time goes:
time: 244 us; the launch traced here: 242 us
  blocking collectives  101 us (41%)
  other arithmetic  41.5 us (17%)
  matrix products  25.3 us (10%)
  local copies, waits for them, and re-layouts  21.2 us (9%)
  waiting for transfers between devices  19.4 us (8%)
  between operations  15.7 us (6%)
  starting transfers between devices  12.4 us (5%)
  loops' own time  5.2 us (2%)
    all_gather x1, blocking collectives, shards(): piece_keys = lax.all_gather(my_keys, 'seq', axis=0, tiled=True)  32.9 us
    all_gather x1, blocking collectives, shards(): piece_values = lax.all_gather(my_values, 'seq', axis=0, tiled=True)  32.9 us
    reduce_scatter x1, waiting for transfers between devices, shards(): lax.psum_scatter(terms.astype(jnp.bfloat16), 'head', scatter_dimension=1,...  19.3 us
    unnamed x1, blocking collectives  18.7 us
    select_n x8, other arithmetic, turn(): return jax.tree.map(lambda a, b: jnp.where(reached, a, b), new, before)  18.1 us
    all_gather x1, blocking collectives, shards(): piece_marks = lax.all_gather(marks, 'seq', axis=0, tiled=True)  16.8 us
    ppermute x3, starting transfers between devices, shifted(): lax.ppermute(value, axis, [(source, source + steps) for source in range(f...  12.4 us
    dot_general x8, matrix products, one_block(): jnp.einsum('hqk,kd->hqd', weights.astype(jnp.bfloat16), block_values, pre...  7.87 us
  transfers between devices with their start and end apart: 5, of which 1 were waited for; matrix products, arithmetic and copies ran while one was open for 24% of the time, Pallas kernels for 0%

commit v1 on v0

--- a/solution.py
+++ b/solution.py
@@ -9,6 +9,18 @@
 QH = 8
 KVH = 2
 HD = 128
+
+
+def collect(value, axis, dim):
+    ways, here, step = (lax.axis_size(axis), lax.axis_index(axis), value.shape[dim])
+    line, have = (value, 1)
+    while have < ways:
+        line = jnp.concatenate(
+            [line, lax.ppermute(line, axis, [(d, (d - have) % ways) for d in range(ways)])],
+            axis=dim,
+        )
+        have = 2 * have
+    return jnp.roll(line, here * step, axis=dim)
 
 
 def shifted(value, axis, steps):
@@ -156,7 +168,7 @@
         jnp.zeros((heads_here, item_count), jnp.float32),
         jnp.zeros((heads_here, item_count, HD), jnp.float32),
     )
-    piece_keys = lax.all_gather(my_keys, "seq", axis=0, tiled=True)
+    piece_keys = collect(my_keys, "seq", 0)
     piece_values = lax.all_gather(my_values, "seq", axis=0, tiled=True)
     piece_marks = lax.all_gather(marks, "seq", axis=0, tiled=True)
     rows = piece_keys.shape[0]

time: 244 us -> 255 us (1.045)
  blocking collectives: 101 us -> 68.5 us
  other arithmetic: 41.5 us -> 63.4 us
  waiting for transfers between devices: 19.4 us -> 29.6 us
  local copies, waits for them, and re-layouts: 21.2 us -> 30.4 us
    all_gather x1 -> x0, blocking collectives: 32.9 us -> none  [shards(): piece_keys = lax.all_gather(my_keys, 'seq', axis=0, tiled=True)]
    convert_element_type x8, other arithmetic: 0.04 us -> 10.3 us  [turn(): part[k].astype(own.dtype)]
    add x8, other arithmetic: 0.14 us -> 9.6 us  [one_block(): total = total * rescale + jnp.sum(weights, axis=-1)]
    ppermute x0 -> x3, waiting for transfers between devices: none -> 6.91 us  [collect(): lax.ppermute(line, axis, [(d, (d - have) % ways) for d in range(ways)])]
    unnamed x30 -> x33, local copies, waits for them, and re-layouts: 6.8 us -> 10.8 us
  transfers between devices with their start and end apart: 5 -> 8, of which waited for: 1 -> 4; matrix products, arithmetic and copies ran while one was open for 24% -> 33% of each run, Pallas kernels for 0% -> 0%
where the time goes in v1:
time: 255 us; the launch traced here: 252 us
  blocking collectives  68.5 us (27%)
  other arithmetic  63.4 us (25%)
  local copies, waits for them, and re-layouts  30.4 us (12%)
  waiting for transfers between devices  29.6 us (12%)
  matrix products  26.5 us (10%)
  between operations  15.5 us (6%)
  starting transfers between devices  12.8 us (5%)
  loops' own time  5.08 us (2%)
    all_gather x1, blocking collectives, shards(): piece_values = lax.all_gather(my_values, 'seq', axis=0, tiled=True)  32.8 us
    reduce_scatter x1, waiting for transfers between devices, shards(): lax.psum_scatter(terms.astype(jnp.bfloat16), 'head', scatter_dimension=1,...  20.6 us
    all_gather x1, blocking collectives, shards(): piece_marks = lax.all_gather(marks, 'seq', axis=0, tiled=True)  18.5 us
    select_n x8, other arithmetic, turn(): return jax.tree.map(lambda a, b: jnp.where(reached, a, b), new, before)  18.2 us
    unnamed x1, blocking collectives  17.2 us
    ppermute x3, starting transfers between devices, shifted(): lax.ppermute(value, axis, [(source, source + steps) for source in range(f...  12.4 us
    unnamed x33, local copies, waits for them, and re-layouts  10.8 us
    convert_element_type x8, other arithmetic, turn(): part[k].astype(own.dtype)  10.3 us
  transfers between devices with their start and end apart: 8, of which 4 were waited for; matrix products, arithmetic and copies ran while one was open for 33% of the time, Pallas kernels for 0%

profile of v1, /device:TPU:0, one launch (start us, length us, event | category | flops | bytes accessed | tf_op | source)
XLA Modules:
  0.0 251.7 jit_solution(2249490985111721678)
XLA Ops:
  6.5 1.4 fusion.75
  8.5 5.4 %collective-permute-start.1 = (bf16[3]{0:T(256)(128)(2,1)}, bf16[3]{0:T(256)(128)(2,1)}, u32[]{:S(2)}, u32[]{:S(2)}) collective-permute-start(bf16[3]{0:T(256)(128)(2,1)} %slice.85), channel_id=1, source_target_pairs={{0,4},{4,8},{8,12},{12,16},{16,20},{20,24},{24,28},{1,5},{5,9},{9,... | collective-permute-start | bytes 26 | tf_op jit(solution)/shard_map/ppermute | solution.py:29
  13.9 1.3 slice.95
  15.2 3.5 %collective-permute-start.2 = (bf16[3,512]{1,0:T(4,128)(2,1)}, bf16[3,512]{1,0:T(4,128)(2,1)}, u32[]{:S(2)}, u32[]{:S(2)}) collective-permute-start(bf16[3,512]{1,0:T(4,128)(2,1)} %slice.95), channel_id=1, source_target_pairs={{0,4},{4,8},{8,12},{12,16},{16,20},{20,24},{24,28},{1,5},{5,9},{9,... | collective-permute-start | bytes 9224 | tf_op jit(solution)/shard_map/ppermute | solution.py:29
  20.3 3.5 %collective-permute-start = (bf16[3,768]{0,1:T(8,128)(2,1)}, bf16[3,768]{0,1:T(8,128)(2,1)}, u32[]{:S(2)}, u32[]{:S(2)}) collective-permute-start(bf16[3,768]{0,1:T(8,128)(2,1)} %copy.27), channel_id=1, source_target_pairs={{0,4},{4,8},{8,12},{12,16},{16,20},{20,24},{24,28},{1,5},{5,9},{9,... | collective-permute-start | bytes 13832 | tf_op jit(solution)/shard_map/ppermute | solution.py:29
  23.8 1.4 constant_dynamic-update-slice_fusion.7
  25.2 1.2 slice.106
  26.4 1.6 convert_element_type.131
  28.0 1.1 copy.28
  29.1 1.4 fusion.64
  30.5 1.5 fusion.74
  32.0 1.5 slice_reduce_fusion.4
  34.9 1.4 fusion.71
  37.3 1.1 copy.29
  39.2 1.3 mul.346
  41.3 32.8 %all_gather.20 = bf16[1024,128]{1,0:T(8,128)(2,1)} all-gather(bf16[128,128]{1,0:T(8,128)(2,1)S(1)} %constant_dynamic-slice_fusion.1), channel_id=1, replica_groups=mesh['seq'=8,'head'=4] {'seq'}, dimensions={0}, use_global_device_ids=true | all-gather | bytes 294912 | tf_op jit(solution)/shard_map/all_gather | solution.py:172
  74.2 18.5 %all-gather.2 = bf16[8,1,128]{2,1,0:T(2,128)(2,1)S(1)} all-gather(bf16[1,1,128]{2,1,0:T(2,128)(2,1)} %get-tuple-element.297), channel_id=1, replica_groups=mesh['seq'=8,'head'=4] {'seq'}, dimensions={0}, use_global_device_ids=true | all-gather | bytes 2304 | tf_op jit(solution)/shard_map/all_gather | solution.py:173
  94.3 1.3 dynamic-slice
  98.8 1.3 compare_convert_fusion.4
  100.0 1.3 multiply_bitcast_fusion.1
  101.8 17.2 %all-reduce = bf16[96]{0:T(256)(128)(2,1)S(1)} all-reduce(bf16[96]{0:T(256)(128)(2,1)S(1)} %dynamic-update-slice), channel_id=2, replica_groups=mesh['seq'=8,'head'=4] {'seq'}, use_global_device_ids=true, to_apply=%add | all-reduce | flops 96 | bytes 384
  120.3 1.5 multiply_convert_fusion.2
  123.6 2.5 %multiply_convert_fusion.1 = bf16[128,768]{0,1:T(8,128)(2,1)S(1)} fusion(f32[128,768]{0,1:T(8,128)} %convert_element_type.121, f32[3,768]{0,1:T(8,128)S(1)} %convert_element_type.120, f32[768]{0:T(1024)} %get-tuple-element.241, f32[128]{0:T(128)S(1)} %get-tuple-element.292, f32[768]{0:T(1024)} %get-tuple-element.242, f32[128]{0:T(128)S(1)} %get-tuple-element.293, ...), kind=kLoop, calls=%fused_computation.74 | loop fusion | flops 1769472 | bytes 612864 | tf_op jit(solution)/shard_map/convert_element_type | solution.py:64
  126.8 1.9 convolution_convert_fusion
  128.8 1.6 collective-permute-done.4
  131.8 5.3 %collective-permute-done.5 = bf16[512,128]{1,0:T(8,128)(2,1)S(1)} collective-permute-done((bf16[512,128]{1,0:T(8,128)(2,1)S(1)}, bf16[512,128]{1,0:T(8,128)(2,1)S(1)}, u32[]{:S(2)}, u32[]{:S(2)}) %collective-permute-start.5) | collective-permute-done | bytes 131104 | tf_op jit(solution)/shard_map/ppermute | solution.py:19
  140.2 1.7 constant_dynamic-slice_fusion.2
  141.8 41.7 %while.30 = (s32[]{:T(128)}, f32[2,128]{1,0:T(2,128)S(1)}, f32[2,128]{1,0:T(2,128)}, f32[2,128,128]{2,1,0:T(8,128)S(1)}, bf16[8,128]{1,0:T(8,128)(2,1)}, /*index...) while((s32[]{:T(128)}, f32[2,128]{1,0:T(2,128)S(1)}, ...), condition=%wide.region_7.8_spmd.clone, body=%wide.region_4.7_spmd.clone.sunk | while | flops 17172484 | bytes 840889 | solution.py:211
  145.4 1.0 convolution_add_fusion.3
  149.5 1.3 fusion.100
  150.7 1.0 convolution_add_fusion.3
  154.8 1.3 fusion.100
  156.0 1.0 convolution_add_fusion.3
  160.1 1.3 fusion.100
  161.3 1.0 convolution_add_fusion.3
  165.3 1.3 fusion.100
  166.6 1.0 convolution_add_fusion.3
  170.6 1.3 fusion.100
  171.9 1.0 convolution_add_fusion.3
  175.9 1.3 fusion.100
  181.2 1.3 fusion.100
  184.3 2.5 %fusion.76 = f32[128,2048]{1,0:T(8,128)} fusion(bf16[128,256]{0,1:T(8,128)(2,1)S(1)} %bitcast.93, bf16[256,2048]{1,0:T(8,128)(2,1)} %param.33), kind=kOutput, calls=%fused_computation.143 | convolution fusion | flops 134217728 | bytes 2162688 | tf_op jit(solution)/shard_map/dot_general | solution.py:219
  186.9 2.1 all-gather.5.cloned.1.call-done
  188.9 28.5 %while.29 = (s32[]{:T(128)}, f32[12,64,256]{2,1,0:T(8,128)}, s32[]{:T(128)}, bf16[8,12]{1,0:T(8,128)(2,1)}, bf16[8,12,64,256]{3,2,1,0:T(8,128)(2,1)}, /*index=5*/s32[]{:T(128)}, s32[]{:T(128)}) while((s32[]{:T(128)}, f32[12,64,256]{2,1,0:T(8,128)}, s32[]{:T(128)}, bf16[8,12]{1,0:T(8,128)(2,1)}, bf16[8,12,64,256]{3,2,1,0:T(8,128)(2,1)}, ...), condition=%wide.region_2.3_spmd.clone, body=%wide.region_1.2_spmd.clone.sunk | while | flops 983056 | bytes 1966305 | solution.py:52
  188.9 1.3 bitcast_convert_fusion.2
  190.3 2.1 fusion.92
  192.3 1.3 bitcast_convert_fusion.2
  193.6 2.3 fusion.92
  195.9 1.3 bitcast_convert_fusion.2
  197.2 2.3 fusion.92
  199.5 1.3 bitcast_convert_fusion.2
  200.8 2.3 fusion.92
  203.1 1.3 bitcast_convert_fusion.2
  204.4 2.3 fusion.92
  206.7 1.3 bitcast_convert_fusion.2
  208.0 2.3 fusion.92
  210.3 1.3 bitcast_convert_fusion.2
  211.6 2.3 fusion.92
  213.9 1.3 bitcast_convert_fusion.2
  215.2 2.3 fusion.92
  217.5 1.7 convolution_multiply_fusion.1
  219.2 2.7 %multiply_reduce_fusion = (f32[128,12]{0,1:T(8,128)S(1)}, f32[128,12,64]{0,2,1:T(8,128)S(1)}) fusion(f32[128,12,64]{0,2,1:T(8,128)} %bitcast.92, f32[128,12,64]{0,2,1:T(8,128)S(1)} %convolution_multiply_fusion.1, f32[12,128]{1,0:T(8,128)S(1)} %reduce_window_sum.11, f32[128,128]{1,0:T(8,128)S(1)} %copy-done.6, pred[128,128]{1,0:T(8,128)(4,1)} %fusion.64, ...), kind=kOutput, calls=%fused_computation.69 | convolution fusion | flops 152173056 | bytes 1476608 | tf_op jit(solution)/shard_map/htj,jhd->thd/dot_general | solution.py:78
  222.8 1.4 fusion.20
  224.3 20.6 %reduce-scatter.2.cloned.1.call-done = bf16[128,512]{1,0:T(8,128)(2,1)} async-done(((bf16[128,2048]{1,0:T(8,128)(2,1)}), bf16[128,512]{1,0:T(8,128)(2,1)}) %reduce-scatter.2.cloned.1.call-update) | async-done | bytes 131088 | tf_op jit(solution)/shard_map/reduce_scatter | solution.py:222
  (144 shorter events, 41.5 us)
Async XLA Ops:
  6.5 216.3 %copy-start = (bf16[768,2048]{1,0:T(8,128)(2,1)S(1)}, bf16[768,2048]{1,0:T(8,128)(2,1)}, u32[]{:S(2)}) copy-start(bf16[768,2048]{1,0:T(8,128)(2,1)} %param.32) | copy-start | bytes 9437188
  6.5 91.0 %copy-start.7 = (s32[128]{0:T(128)S(1)}, s32[128]{0:T(128)}, u32[]{:S(2)}) copy-start(s32[128]{0:T(128)} %param.31) | copy-start | bytes 1540
  6.5 182.4 %all-gather.5.cloned.1.call-start = ((), (), s32[]{:S(2)}) async-start(), calls=%async_computation.2 | async-start | bytes 3538944 | tf_op jit(solution)/shard_map/all_gather | solution.py:35
  8.5 87.7 %collective-permute-start.1 = (bf16[3]{0:T(256)(128)(2,1)}, bf16[3]{0:T(256)(128)(2,1)}, u32[]{:S(2)}, u32[]{:S(2)}) collective-permute-start(bf16[3]{0:T(256)(128)(2,1)} %slice.85), channel_id=1, source_target_pairs={{0,4},{4,8},{8,12},{12,16},{16,20},{20,24},{24,28},{1,5},{5,9},{9,... | collective-permute-start | bytes 26 | tf_op jit(solution)/shard_map/ppermute | solution.py:29
  15.2 104.4 %collective-permute-start.2 = (bf16[3,512]{1,0:T(4,128)(2,1)}, bf16[3,512]{1,0:T(4,128)(2,1)}, u32[]{:S(2)}, u32[]{:S(2)}) collective-permute-start(bf16[3,512]{1,0:T(4,128)(2,1)} %slice.95), channel_id=1, source_target_pairs={{0,4},{4,8},{8,12},{12,16},{16,20},{20,24},{24,28},{1,5},{5,9},{9,... | collective-permute-start | bytes 9224 | tf_op jit(solution)/shard_map/ppermute | solution.py:29
  20.3 102.3 %collective-permute-start = (bf16[3,768]{0,1:T(8,128)(2,1)}, bf16[3,768]{0,1:T(8,128)(2,1)}, u32[]{:S(2)}, u32[]{:S(2)}) collective-permute-start(bf16[3,768]{0,1:T(8,128)(2,1)} %copy.27), channel_id=1, source_target_pairs={{0,4},{4,8},{8,12},{12,16},{16,20},{20,24},{24,28},{1,5},{5,9},{9,... | collective-permute-start | bytes 13832 | tf_op jit(solution)/shard_map/ppermute | solution.py:29
  25.2 100.9 %collective-permute-start.3 = (bf16[128,128]{1,0:T(8,128)(2,1)S(1)}, bf16[128,128]{1,0:T(8,128)(2,1)S(1)}, u32[]{:S(2)}, u32[]{:S(2)}) collective-permute-start(bf16[128,128]{1,0:T(8,128)(2,1)S(1)} %get-tuple-element.278), channel_id=1, source_target_pairs={{0,28},{4,0},{8,4},{12,8},{16,12},{20,16},{24,20},{28,24},{1,29},{... | collective-permute-start | bytes 98312 | tf_op jit(solution)/shard_map/ppermute | solution.py:19
  121.8 4.6 %copy-start.2 = (bf16[128,512]{1,0:T(8,128)(2,1)}, bf16[128,512]{1,0:T(8,128)(2,1)S(1)}, u32[]{:S(2)}) copy-start(bf16[128,512]{1,0:T(8,128)(2,1)S(1)} %multiply_convert_fusion.2) | copy-start | bytes 393220
  126.1 0.7 copy-start.4
  126.1 4.3 %collective-permute-start.4 = (bf16[256,128]{1,0:T(8,128)(2,1)S(1)}, bf16[256,128]{1,0:T(8,128)(2,1)S(1)}, u32[]{:S(2)}, u32[]{:S(2)}) collective-permute-start(bf16[256,128]{1,0:T(8,128)(2,1)S(1)} %pad_maximum_fusion.3), channel_id=1, source_target_pairs={{0,24},{4,28},{8,0},{12,4},{16,8},{20,12},{24,16},{28,20},{1,25},{... | collective-permute-start | bytes 196616 | tf_op jit(solution)/shard_map/ppermute | solution.py:19
  128.7 116.1 %reduce-scatter.2.cloned.1.call-start = ((), (), s32[]{:S(2)}) async-start(), calls=%async_computation.1 | async-start | bytes 655360 | tf_op jit(solution)/shard_map/reduce_scatter | solution.py:222
  130.5 6.6 %collective-permute-start.5 = (bf16[512,128]{1,0:T(8,128)(2,1)S(1)}, bf16[512,128]{1,0:T(8,128)(2,1)S(1)}, u32[]{:S(2)}, u32[]{:S(2)}) collective-permute-start(bf16[512,128]{1,0:T(8,128)(2,1)S(1)} %pad_maximum_fusion.2), channel_id=1, source_target_pairs={{0,16},{4,20},{8,24},{12,28},{16,0},{20,4},{24,8},{28,12},{1,17},{... | collective-permute-start | bytes 393224 | tf_op jit(solution)/shard_map/ppermute | solution.py:19
  188.9 28.5 %copy-start.3 = (bf16[128,512]{1,0:T(8,128)(2,1)S(1)}, bf16[128,512]{1,0:T(8,128)(2,1)}, u32[]{:S(2)}) copy-start(bf16[128,512]{1,0:T(8,128)(2,1)} %copy-done.2) | copy-start | bytes 393220
  188.9 30.3 %copy-start.5 = (bf16[128,768]{0,1:T(8,128)(2,1)S(1)}, bf16[128,768]{0,1:T(8,128)(2,1)}, u32[]{:S(2)}) copy-start(bf16[128,768]{0,1:T(8,128)(2,1)} %copy-done.4) | copy-start | bytes 589828
  188.9 30.3 %copy-start.6 = (f32[128,128]{1,0:T(8,128)S(1)}, f32[128,128]{1,0:T(8,128)}, u32[]{:S(2)}) copy-start(f32[128,128]{1,0:T(8,128)} %fusion.66) | copy-start | bytes 196612
  188.9 30.3 %copy-start.8 = (f32[128,12]{0,1:T(8,128)S(1)}, f32[128,12]{0,1:T(8,128)}, u32[]{:S(2)}) copy-start(f32[128,12]{0,1:T(8,128)} %get-tuple-element.283) | copy-start | bytes 18436
  217.5 5.4 %copy-start.1 = (f32[128,2048]{1,0:T(8,128)S(1)}, f32[128,2048]{1,0:T(8,128)}, u32[]{:S(2)}) copy-start(f32[128,2048]{1,0:T(8,128)} %fusion.76) | copy-start | bytes 3145732
Sparse Core Ops, SparseCore 0:
  128.9 60.0 all-gather.4
  224.4 20.4 reduce-scatter.1
